TPU v7x, 256 devices: a whole 4x4x8 slice. The times are simulated.
256 devices in a mesh: outer: 16 (over y_lo, x, core), node: 16 (over y_hi, z).
Axes of the slice: x: 4, y: 4 (y_hi: 2, y_lo: 2; y = y_hi * 2 + y_lo), z: 8, core: 2. Of those that a mesh axis runs over, the one named last changes fastest.
Arguments:
- tokens: bfloat16 [65536, 14848], P(('outer', 'node')), may hold values from -24 to 24
- cotangent: bfloat16 [65536, 256], P(('outer', 'node')), may hold values from -0.0234375 to 0.0234375
- weight_codes: bfloat16 [14848, 256], P('node'), may hold values from -127 to 127, as said below
- weight_scales: float32 [14848, 2], P('node'), may hold values from 4.103326e-05 to 0.00024619958
- weight_bits: int32 [256], replicated, may hold values 0 or 1
- grad_bits: int32 [256], replicated, may hold values 0 or 1
Outputs:
- output: bfloat16 [65536, 256], P(('outer', 'node'))
- grad_rotated: float32 [14848, 256], P(('outer', 'node'))
Inputs may be any that keep to these rules, and one draw needn't show every extreme that they name: `weight_codes`: whole numbers.
All inputs are finite; a program needn't handle non-finite values.
Results may differ from a plain program's by a relative error of at most 0.015.
Values may be sent and summed in bfloat16 or wider, within the bound.
A program may use at most 128 MiB of HBM per device.

v0:
```python
import math

import jax
import jax.numpy as jnp
import numpy as np
from jax import lax
from jax.sharding import PartitionSpec as P


def sylvester():
    row_index = np.arange(128).reshape(128, 1)
    column_index = np.arange(128).reshape(1, 128)
    parity = np.zeros((128, 128))
    for level in range(7):
        parity = parity + row_index // 2**level % 2 * (column_index // 2**level % 2)
    return 1.0 - 2.0 * (parity % 2)


def rotate(values, bits):
    height, width = values.shape
    signs = (2 * bits - 1).astype(jnp.float32)
    table = jnp.asarray(sylvester(), jnp.float32) / math.sqrt(128.0)
    blocks = (values * signs).reshape(height, width // 128, 128)
    return jnp.einsum("rbi,ij->rbj", blocks, table, precision=lax.Precision.HIGHEST).reshape(
        height, width
    )


def dequantize(codes, scales):
    height, width = codes.shape
    blocks = codes.astype(jnp.float32).reshape(height, width // 128, 128)
    return (blocks * scales[:, :, None]).reshape(height, width)


def weight_term(source, cotangent):
    return lax.dot_general(
        source, cotangent, (((0,), (0,)), ((), ())), preferred_element_type=jnp.float32
    )


def on_device(tokens, cotangent, weight_codes, weight_scales, weight_bits, grad_bits):
    tok_rows, width = tokens.shape
    n_outer = lax.axis_size("outer")
    n_node = lax.axis_size("node")
    share = width // (n_outer * n_node)
    codes = lax.all_gather(weight_codes, "node", axis=0, tiled=True)
    scales = lax.all_gather(weight_scales.astype(jnp.bfloat16), "node", axis=0, tiled=True).astype(
        jnp.float32
    )
    built = rotate(dequantize(codes, scales), weight_bits).astype(jnp.bfloat16)
    summed = jnp.dot(tokens, built, preferred_element_type=jnp.float32)
    output = summed.astype(jnp.bfloat16)
    arranged = (
        tokens.reshape(tok_rows, n_outer, n_node, share)
        .transpose(0, 2, 1, 3)
        .reshape(tok_rows, width)
    )
    term = weight_term(arranged, cotangent)
    term = rotate(term, grad_bits)
    within = lax.psum_scatter(term, "node", scatter_dimension=0, tiled=True)
    reduced = lax.psum_scatter(within, "outer", scatter_dimension=0, tiled=True)
    return (output, reduced)


def solution(mesh):
    return jax.shard_map(
        on_device,
        mesh=mesh,
        in_specs=(
            P(("outer", "node"), None),
            P(("outer", "node"), None),
            P("node", None),
            P("node", None),
            P(),
            P(),
        ),
        out_specs=(P(("outer", "node"), None), P(("outer", "node"), None)),
        check_vma=False,
    )
```

profile of v0, /device:TPU:1, one launch (start us, length us, event | category | flops | bytes accessed | tf_op | source)
XLA Modules:
  0.0 473.7 jit_solution(13792835973148870908)
XLA Ops:
  7.2 0.0 copy-start
  7.2 0.0 all-gather.3.cloned.1.call-start
  7.2 0.7 all-gather.3.cloned.1.call-update
  7.9 0.0 reduce-scatter.4.cloned.1.call-start
  8.0 10.3 %copy.33 = bf16[256,14848]{0,1:T(8,128)(2,1)} copy(bf16[256,14848]{1,0:T(8,128)(2,1)} %param.8) | data formatting | bytes 15204352 | tf_op args[0]
  18.2 11.3 %reshape.28 = bf16[256,16,16,58]{0,3,2,1:T(8,128)(2,1)} reshape(bf16[256,14848]{0,1:T(8,128)(2,1)} %copy.33) | data formatting | bytes 15204352 | tf_op jit(solution)/shard_map/reshape | solution.py:54
  29.6 8.3 %copy.34 = bf16[256,16,16,58]{0,3,2,1:T(8,128)(2,1)} copy(bf16[256,16,16,58]{0,3,1,2:T(8,128)(2,1)} %bitcast.43) | data formatting | bytes 15204352 | tf_op jit(solution)/shard_map/transpose | solution.py:55
  37.9 11.3 %reshape.29 = bf16[256,14848]{0,1:T(8,128)(2,1)} reshape(bf16[256,16,16,58]{0,3,2,1:T(8,128)(2,1)} %copy.34) | data formatting | bytes 15204352 | tf_op jit(solution)/shard_map/reshape | solution.py:56
  49.2 5.4 %convolution_multiply_fusion = f32[14848,256]{0,1:T(8,128)S(1)} fusion(bf16[256,14848]{0,1:T(8,128)(2,1)} %reshape.29, bf16[256,256]{1,0:T(8,128)(2,1)S(1)} %copy-done, f32[256]{0:T(256)S(1)} %add_convert_fusion), kind=kOutput, calls=%fused_computation.1 | convolution fusion | flops 1949958144 | bytes 22938624 | tf_op jit(solution)/shard_map/dot_general | solution.py:36
  54.6 0.0 copy-done.2
  54.6 16.6 %fusion.6 = f32[14848,2,128]{0,2,1:T(8,128)} fusion(f32[14848,2,128]{0,2,1:T(8,128)S(1)} %bitcast.41, f32[128,128,1]{0,1,2:T(8,128)S(1)} %copy-done.2), kind=kOutput, calls=%fused_computation.14 | convolution fusion | flops 5838471168 | bytes 30474240 | tf_op jit(solution)/shard_map/rbi,ij->rbj/dot_general | solution.py:24
  71.3 15.5 %copy.36 = f32[14848,256]{1,0:T(8,128)} copy(f32[14848,256]{0,1:T(8,128)} %bitcast.42) | data formatting | bytes 30408704 | tf_op jit(solution)/shard_map/reshape | solution.py:24
  86.7 0.0 reduce-scatter.4.cloned.1.call-update
  86.8 0.7 copy-done.3
  87.4 39.0 %all-gather = bf16[16,928,2]{1,2,0:T(2,128)(2,1)S(1)} all-gather(bf16[1,928,2]{1,2,0:T(2,128)(2,1)S(1)} %convert_bitcast_fusion), channel_id=1, replica_groups=mesh['outer'=16,'node'=16] {'node'}, dimensions={0}, use_global_device_ids=true | all-gather | bytes 63104 | tf_op jit(solution)/shard_map/all_gather | solution.py:47
  126.4 4.6 copy.39
  131.0 0.6 dynamic-slice.4
  132.3 10.5 %all-gather.3.cloned.1.call-done = bf16[14848,256]{1,0:T(8,128)(2,1)} async-done(((bf16[928,256]{1,0:T(8,128)(2,1)}), bf16[14848,256]{1,0:T(8,128)(2,1)}) %all-gather.3.cloned.1.call-update) | async-done | bytes 7602192 | tf_op jit(solution)/shard_map/all_gather | solution.py:46
  142.8 28.8 %mul.33 = f32[14848,2,128]{2,1,0:T(2,128)} broadcast(f32[14848,2]{1,0:T(8,128)} %bitcast.46), dimensions={0,1} | broadcast | bytes 15323136 | tf_op jit(solution)/shard_map/mul | solution.py:32
  171.6 0.0 slice-done
  171.6 0.0 copy-start.1
  171.6 22.2 %convolution_convert_fusion = bf16[14848,2,128]{0,2,1:T(8,128)(2,1)} fusion(f32[128,128,1]{0,1,2:T(8,128)S(1)} %copy-done.2, f32[1856,8,2,128]{3,2,1,0:T(2,128)} %bitcast.40, bf16[14848,256]{1,0:T(8,128)(2,1)S(1)} %bitcast.45, f32[256]{0:T(256)S(1)} %add_convert_fusion.1), kind=kOutput, calls=%fused_computation | convolution fusion | flops 5853675520 | bytes 30475264 | tf_op jit(solution)/shard_map/rbi,ij->rbj/dot_general | solution.py:24
  193.8 225.6 %reduce-scatter.4.cloned.1.call-done = f32[928,256]{1,0:T(8,128)} async-done(((f32[14848,256]{1,0:T(8,128)}), f32[928,256]{1,0:T(8,128)}) %reduce-scatter.4.cloned.1.call-update) | async-done | bytes 950288 | tf_op jit(solution)/shard_map/reduce_scatter | solution.py:60
  419.3 35.0 %fusion = f32[64,256]{1,0:T(8,128)S(1)} fusion(f32[928,256]{1,0:T(8,128)} %reduce-scatter.4.cloned.1.call-done), kind=kCustom, calls=%all-reduce-scatter | all-reduce-scatter fusion | flops 262145 | bytes 1016832
  454.3 1.9 collective-permute-start
  456.3 1.3 collective-permute-start.1
  457.6 7.5 %fusion.5 = bf16[256,256]{0,1:T(8,128)(2,1)S(1)} fusion(bf16[14848,256]{0,1:T(8,128)(2,1)} %bitcast.47, bf16[256,14848]{1,0:T(8,128)(2,1)} %param.8), kind=kOutput, calls=%fused_computation.8 | convolution fusion | flops 1946222592 | bytes 15335424 | tf_op jit(solution)/shard_map/dot_general | solution.py:51
  465.1 0.8 copy.37
  465.8 0.0 collective-permute-done.1
  465.8 0.0 collective-permute-done
  465.8 0.4 concatenate
  466.2 0.6 constant_dynamic-slice_fusion
  (19 shorter events, 0.1 us)
Async XLA Ops:
  7.2 42.0 %copy-start = (bf16[256,256]{1,0:T(8,128)(2,1)S(1)}, bf16[256,256]{1,0:T(8,128)(2,1)}, u32[]{:S(2)}) copy-start(bf16[256,256]{1,0:T(8,128)(2,1)} %param.9) | copy-start | bytes 393220
  7.2 135.6 %all-gather.3.cloned.1.call-start = ((), (), s32[]{:S(2)}) async-start(), calls=%async_computation.1 | async-start | bytes 8077312 | tf_op jit(solution)/shard_map/all_gather | solution.py:46
  7.9 411.4 %reduce-scatter.4.cloned.1.call-start = ((), (), s32[]{:S(2)}) async-start(), calls=%async_computation.2 | async-start | bytes 16154624 | tf_op jit(solution)/shard_map/reduce_scatter | solution.py:60
  29.6 19.6 %copy-start.4 = (s32[256]{0:T(256)S(1)}, s32[256]{0:T(256)}, u32[]{:S(2)}) copy-start(s32[256]{0:T(256)} %param.13) | copy-start | bytes 3076
  49.2 5.5 %copy-start.2 = (f32[128,128,1]{0,1,2:T(8,128)S(1)}, f32[128,128,1]{0,1,2:T(8,128)}, u32[]{:S(2)}) copy-start(f32[128,128,1]{0,1,2:T(8,128)} %constant.18) | copy-start | bytes 196612
  86.7 0.7 copy-start.3
  86.7 44.2 %copy-start.6 = (u32[256]{0:T(256)S(1)}, u32[256]{0:T(256)}, u32[]{:S(2)}) copy-start(u32[256]{0:T(256)} %constant.16) | copy-start | bytes 3076
  86.7 45.5 %copy-start.5 = (s32[256]{0:T(256)S(1)}, s32[256]{0:T(256)}, u32[]{:S(2)}) copy-start(s32[256]{0:T(256)} %param.12) | copy-start | bytes 3076
  142.8 28.8 %slice-start = ((s8[7602176]{0:T(1024)(128)(4,1)}), s8[4194304]{0:T(1024)(128)(4,1)S(1)}, s32[]{:S(2)}) async-start(s8[7602176]{0:T(1024)(128)(4,1)} %bitcast.44), calls=%async_computation.3 | async-start | bytes 8388608
  142.8 28.8 %slice-start.1 = ((s8[7602176]{0:T(1024)(128)(4,1)}), s8[3407872]{0:T(1024)(128)(4,1)S(1)}, s32[]{:S(2)}) async-start(s8[7602176]{0:T(1024)(128)(4,1)} %bitcast.44), calls=%async_computation.4 | async-start | bytes 6815744
  171.6 295.3 %copy-start.1 = (bf16[256,256]{1,0:T(8,128)(2,1)S(1)}, bf16[256,256]{1,0:T(8,128)(2,1)}, u32[]{:S(2)}) copy-start(bf16[256,256]{1,0:T(8,128)(2,1)} %param.9) | copy-start | bytes 393220
  454.3 11.5 %collective-permute-start = (f32[64,256]{1,0:T(8,128)S(1)}, f32[64,256]{1,0:T(8,128)S(1)}, u32[]{:S(2)}, u32[]{:S(2)}) collective-permute-start(f32[64,256]{1,0:T(8,128)S(1)} %fusion), channel_id=1, source_target_pairs={{0,16},{16,32},{32,48},{48,64},{64,80},{80,96},{96,112},{112,128},... | collective-permute-start | bytes 196616
  456.3 9.6 %collective-permute-start.1 = (f32[26,256]{1,0:T(8,128)S(1)}, f32[26,256]{1,0:T(8,128)S(1)}, u32[]{:S(2)}, u32[]{:S(2)}) collective-permute-start(f32[26,256]{1,0:T(8,128)S(1)} %slice), channel_id=1, source_target_pairs={{0,32},{16,48},{32,64},{48,80},{64,96},{80,112},{96,128},{112,144}... | collective-permute-start | bytes 79880
Sparse Core Ops, SparseCore 0:
  10.6 132.0 all-gather.2
  146.9 272.3 reduce-scatter.3
where the time goes:
time: 479 us; the launch traced here: 474 us
  waiting for transfers between devices  237 us (49%)
  local copies, waits for them, and re-layouts  93.1 us (19%)
  blocking collectives  74 us (15%)
  matrix products  51.7 us (11%)
  between operations  14.8 us (3%)
    reduce_scatter x1, waiting for transfers between devices, on_device(): within = lax.psum_scatter(term, 'node', scatter_dimension=0, tiled=True)  226 us
    all_gather x1, blocking collectives, on_device(): lax.all_gather(weight_scales.astype(jnp.bfloat16), 'node', axis=0, tiled=...  39 us
    dot_general x2, matrix products, rotate(): jnp.einsum('rbi,ij->rbj', blocks, table, precision=lax.Precision.HIGHEST)  38.8 us
    unnamed x1, blocking collectives  35 us
    mul x1, local copies, waits for them, and re-layouts, dequantize(): return (blocks * scales[:, :, None]).reshape(height, width)  28.8 us
    reshape x1, local copies, waits for them, and re-layouts, rotate(): jnp.einsum('rbi,ij->rbj', blocks, table, precision=lax.Precision.HIGHEST)  15.5 us
    unnamed x24, local copies, waits for them, and re-layouts  13.4 us
    reshape x1, local copies, waits for them, and re-layouts, on_device(): tokens.reshape(tok_rows, n_outer, n_node, share).transpose(0, 2, 1, 3)  11.3 us
  transfers between devices with their start and end apart: 4, of which 2 were waited for; matrix products, arithmetic and copies ran while one was open for 30% of the time, Pallas kernels for 0%

commit v1 on v0

v1 whole, which is shorter than its diff:
```python
import math

import jax
import jax.numpy as jnp
import numpy as np
from jax import lax
from jax.experimental import pallas as pl
from jax.experimental.pallas import tpu as pltpu
from jax.sharding import PartitionSpec as P

MESH = pl.DeviceIdType.MESH
SHARD = 928
BLOCK = 58
WIN = 1024
EDGE = 96
ROOT = 1.0 / math.sqrt(128.0)


def sylvester():
    row_index = np.arange(128).reshape(128, 1)
    column_index = np.arange(128).reshape(1, 128)
    parity = np.zeros((128, 128))
    for level in range(7):
        parity = parity + row_index // 2**level % 2 * (column_index // 2**level % 2)
    return 1.0 - 2.0 * (parity % 2)


def kernel(
    tokens, cot_in, codes, scales, wbits, gbits, table,
    out, grad,
    tok, cot, wts, gwin, part, s1, d1, r1, s2, d2, r2, s3, d3, acc, other,
    tok_loc, tok_ss, tok_rs, cot_sem, w_ss, w_rs, ss1, rs1, ss2, rs2, ss3, rs3, o_sem,
):
    o = lax.axis_index("outer")
    n = lax.axis_index("node")
    c = lax.rem(o, 2)
    x = lax.rem(o // 2, 4)
    ylo = o // 8
    yhi = n // 8
    z = lax.rem(n, 8)
    y = yhi * 2 + ylo
    odd = lax.rem(z + c, 2)

    def dev(cc, xx, yy, zz):
        xx, yy, zz = lax.rem(xx + 4, 4), lax.rem(yy + 4, 4), lax.rem(zz + 8, 8)
        return (lax.rem(yy, 2) * 8 + xx * 2 + cc, (yy // 2) * 8 + zz)

    mate = dev(1 - c, x, y, z)
    xp, xm = dev(c, x + 1, y, z), dev(c, x - 1, y, z)
    yp, ym = dev(c, x, y + 1, z), dev(c, x, y - 1, z)
    zp, zm = dev(c, x, y, z + 1), dev(c, x, y, z - 1)
    ypart = dev(c, x, 3 - y, z)

    zero = jnp.zeros((EDGE, 256), jnp.bfloat16)

    @pl.loop(0, 8)
    def _(i):
        wts[i, pl.ds(0, EDGE)] = zero
        wts[i, pl.ds(WIN - EDGE, EDGE)] = zero

    barrier = pltpu.get_barrier_semaphore()
    peers = [mate, xp, xm, yp, ym] + [dev(c, x, y, z + k) for k in range(1, 8)]
    for p in peers:
        pl.semaphore_signal(barrier, inc=1, device_id=p, device_id_type=MESH)

    def start_of(g):
        return pl.multiple_of(g * SHARD - 32 * lax.rem(g, 4), 128)

    def order(i):
        if isinstance(i, int):
            i = jnp.int32(i)
        first = lax.rem(ylo + i, 2) * 4 + lax.rem(x + 2, 4)
        second = ylo * 4 + lax.rem(x + 1 + i, 4)
        third = (1 - ylo) * 4 + lax.rem(x + 2 + i, 4)
        return jnp.where(i < 2, first, jnp.where(i < 5, second, third))

    def local_tok(gi):
        return pltpu.make_async_copy(
            tokens.at[:, pl.ds(start_of(2 * gi + c), WIN)],
            tok.at[gi, pl.ds(pl.multiple_of(c * 256, 256), 256)],
            tok_loc.at[gi],
        )

    def swap_tok(gi):
        return pltpu.make_async_remote_copy(
            src_ref=tokens.at[:, pl.ds(start_of(2 * gi + 1 - c), WIN)],
            dst_ref=tok.at[gi, pl.ds(pl.multiple_of(c * 256, 256), 256)],
            send_sem=tok_ss.at[gi],
            recv_sem=tok_rs.at[gi],
            device_id=mate,
            device_id_type=MESH,
        )

    cot_mine = cot.at[pl.ds(pl.multiple_of(c * 256, 256), 256)]
    local_cot = pltpu.make_async_copy(cot_in, cot_mine, cot_sem.at[0])
    swap_cot = pltpu.make_async_remote_copy(
        src_ref=cot_in, dst_ref=cot_mine, send_sem=cot_sem.at[1], recv_sem=cot_sem.at[2],
        device_id=mate, device_id_type=MESH,
    )
    local_cot.start()

    @pl.loop(0, 8)
    def _(i):
        local_tok(order(i)).start()

    gwin[pl.ds(WIN, EDGE)] = jnp.zeros((EDGE, 256), jnp.float32)
    acc[...] = jnp.zeros_like(acc)

    def shard(yy, zz):
        zz = lax.rem(zz + 8, 8)
        slot = yy * 4 + zz // 2
        return slot, wts.at[slot, pl.ds(pl.multiple_of(32 * lax.rem(zz, 4), 32), SHARD)]

    def push(yy, zz, to, k):
        slot, rows = shard(yy, zz)
        return pltpu.make_async_remote_copy(
            src_ref=rows, dst_ref=rows, send_sem=w_ss.at[k], recv_sem=w_rs.at[slot],
            device_id=to, device_id_type=MESH,
        )

    def arrived(yy, zz):
        push(yy, zz, zp, 0).wait_recv()

    def multiply(yy, zz):
        slot = yy * 4 + lax.rem(zz + 8, 8) // 2
        for half in range(2):
            rows = pl.ds(half * 256, 256)
            acc[rows] += jnp.dot(tok[slot, rows], wts[slot], preferred_element_type=jnp.float32)

    @pl.when(odd == 0)
    def _():
        signs = (2 * wbits[...] - 1).astype(jnp.bfloat16)
        slot = yhi * 4 + z // 2
        base = pl.multiple_of(32 * lax.rem(z, 4), 32)
        for lo in range(0, SHARD, 464):
            for b in range(2):
                cols = pl.ds(b * 128, 128)
                spun = jnp.dot(
                    codes[pl.ds(lo, 464), cols] * signs[:, b * 128:b * 128 + 128], table[...],
                    preferred_element_type=jnp.float32,
                )
                spun = spun * (scales[pl.ds(lo, 464), b:b + 1] * ROOT)
                wts[slot, pl.ds(base + lo, 464), cols] = spun.astype(jnp.bfloat16)

    pl.semaphore_wait(barrier, len(peers))

    swap_cot.start()

    @pl.when(odd == 0)
    def _():
        push(yhi, z, zp, 0).start()
        push(yhi, z, zm, 1).start()
        push(yhi, z, ypart, 2).start()

    @pl.loop(0, 8)
    def _(i):
        swap_tok(order(i)).start()

    local_cot.wait()
    swap_cot.wait_recv()

    def produce(i):
        gi = order(i)
        local_tok(gi).wait()
        swap_tok(gi).wait_recv()
        top = EDGE - 32 * lax.rem(2 * gi + c, 4)

        @pl.loop(0, 4)
        def _(k):
            cols = pl.ds(pl.multiple_of(k * 256, 256), 256)
            piece = lax.dot_general(
                tok[gi, :, cols], cot[...], (((0,), (0,)), ((), ())), preferred_element_type=jnp.float32
            )
            gwin[pl.ds(pl.multiple_of(top + k * 256, 32), 256)] = piece

        for s in range(16):
            for h in range(2):
                part[h, gi, s] = gwin[pl.ds(EDGE + BLOCK * s, 64), pl.ds(h * 128, 128)]

    def ring(level, h):
        along_x = (h == 0) == (level == 1)
        pos = x if along_x else y
        ends = (xp, xm) if along_x else (yp, ym)
        sent, got = (s1, d1) if level == 1 else (s2, d2)
        ssem, rsem = (ss1, rs1) if level == 1 else (ss2, rs2)
        total = r1 if level == 1 else r2

        def copy(way, m):
            return pltpu.make_async_remote_copy(
                src_ref=sent.at[h, way, m], dst_ref=got.at[h, way, m],
                send_sem=ssem.at[h, way, m], recv_sem=rsem.at[h, way, m],
                device_id=ends[way], device_id_type=MESH,
            )

        def read(dest, half, i):
            if level == 1 and h == 0:
                return part[0, half * 4 + dest, i]
            if level == 1:
                return part[1, lax.rem(dest, 2) * 4 + 2 * half + i // 8, (dest // 2) * 8 + lax.rem(i, 8)]
            if h == 0:
                return r1[0, lax.rem(dest, 2) * 16 + (dest // 2) * 8 + half * 4 + i]
            return r1[1, dest * 8 + half * 4 + i]

        count = 16 if level == 1 else 4

        def send(way, m):
            off = (2, 1, 1)[m] if way == 0 else (2, 3, 3)[m]
            dest = lax.rem(pos + off, 4)
            half = (0, 1, 0)[m] if way == 0 else (1, 0, 1)[m]
            if m == 2:
                copy(way, 0).wait_recv()

            @pl.loop(0, count)
            def _(i):
                value = read(dest, half, i)
                if m == 2:
                    value = value + got[h, way, 0, i].astype(jnp.float32)
                sent[h, way, m, i] = value.astype(jnp.bfloat16)

            copy(way, m).start()

        def finish():
            for half in range(2):
                a, b = ((0, 2), (1, 1)) if half == 0 else ((0, 1), (1, 2))
                copy(*b).wait_recv()
                copy(*a).wait_recv()

                @pl.loop(0, count)
                def _(i):
                    value = (
                        read(pos, half, i)
                        + got[(h,) + a + (i,)].astype(jnp.float32)
                        + got[(h,) + b + (i,)].astype(jnp.float32)
                    )
                    if level == 1:
                        r1[h, half * 16 + i] = value
                    else:
                        r2[half * 4 + i, h] = value

        def drain():
            for way in range(2):
                for m in range(3):
                    copy(way, m).wait_send()

        return send, finish, drain

    send_a, finish_a, drain_a = ring(1, 0)
    send_b, finish_b, drain_b = ring(1, 1)
    send_c, finish_c, drain_c = ring(2, 0)
    send_d, finish_d, drain_d = ring(2, 1)

    pl.loop(0, 2)(produce)
    send_a(0, 0)
    send_a(1, 0)
    pl.loop(2, 5)(produce)
    send_b(0, 0)
    send_b(1, 0)

    near, far = yhi, 1 - yhi

    @pl.when(odd == 0)
    def _():
        arrived(far, z)
        push(far, z, zp, 3).start()
        push(far, z, zm, 4).start()

    @pl.when(odd == 1)
    def _():
        arrived(near, z - 1)
        push(near, z - 1, zp, 0).start()
        arrived(near, z + 1)
        push(near, z + 1, zm, 1).start()

    pl.loop(5, 8)(produce)
    send_a(0, 1)
    send_a(1, 1)
    send_b(0, 1)
    send_b(1, 1)
    send_a(0, 2)
    send_a(1, 2)

    @pl.when(odd == 0)
    def _():
        multiply(near, z)
        multiply(far, z)

    @pl.when(odd == 1)
    def _():
        arrived(far, z - 1)
        push(far, z - 1, zp, 2).start()
        arrived(far, z + 1)
        push(far, z + 1, zm, 3).start()
        multiply(near, z - 1)
        multiply(near, z + 1)

    send_b(0, 2)
    send_b(1, 2)

    @pl.when(odd == 0)
    def _():
        arrived(near, z - 2)
        push(near, z - 2, zp, 5).start()
        arrived(near, z + 2)
        push(near, z + 2, zm, 6).start()

    finish_a()
    send_c(0, 0)
    send_c(1, 0)
    send_c(0, 1)
    send_c(1, 1)

    @pl.when(odd == 0)
    def _():
        arrived(far, z - 2)
        push(far, z - 2, zp, 7).start()
        arrived(far, z + 2)
        push(far, z + 2, zm, 8).start()
        multiply(near, z - 2)
        multiply(near, z + 2)

    @pl.when(odd == 1)
    def _():
        arrived(near, z - 3)
        push(near, z - 3, zp, 4).start()
        multiply(far, z - 1)
        multiply(far, z + 1)

    finish_b()
    send_d(0, 0)
    send_d(1, 0)
    send_d(0, 1)
    send_d(1, 1)
    send_c(0, 2)
    send_c(1, 2)
    finish_c()
    send_d(0, 2)
    send_d(1, 2)

    @pl.when(odd == 1)
    def _():
        arrived(far, z + 3)
        push(far, z + 3, zm, 5).start()
        arrived(near, z + 3)
        multiply(near, z - 3)
        multiply(near, z + 3)

    finish_d()

    def last(k):
        to = lax.rem(z + k, 8)
        return pltpu.make_async_remote_copy(
            src_ref=s3.at[to], dst_ref=d3.at[k - 1], send_sem=ss3.at[k - 1], recv_sem=rs3.at[k - 1],
            device_id=dev(c, x, y, z + k), device_id_type=MESH,
        )

    for i in range(8):
        s3[i] = r2[i].astype(jnp.bfloat16)
    for k in (4, 3, 5, 2, 6, 1, 7):
        last(k).start()

    @pl.when(odd == 0)
    def _():
        multiply(far, z - 2)
        multiply(far, z + 2)
        arrived(near, z + 4)
        multiply(near, z + 4)
        arrived(far, z + 4)
        multiply(far, z + 4)

    @pl.when(odd == 1)
    def _():
        arrived(far, z - 3)
        multiply(far, z - 3)
        multiply(far, z + 3)

    theirs = pl.ds(pl.multiple_of((1 - c) * 256, 256), 256)
    mine = pl.ds(pl.multiple_of(c * 256, 256), 256)
    swap_out = pltpu.make_async_remote_copy(
        src_ref=acc.at[theirs], dst_ref=other, send_sem=o_sem.at[0], recv_sem=o_sem.at[1],
        device_id=mate, device_id_type=MESH,
    )
    swap_out.start()

    for k in range(1, 8):
        last(k).wait_recv()
    gsigns = (2 * gbits[...] - 1).astype(jnp.float32)
    for h in range(2):
        value = r2[z, h]
        for k in range(1, 8):
            value = value + d3[k - 1, h].astype(jnp.float32)
        value = value * gsigns[:, h * 128:h * 128 + 128]
        spun = jnp.zeros((64, 128), jnp.float32)
        for _ in range(3):
            head = value.astype(jnp.bfloat16)
            spun = spun + jnp.dot(head, table[...], preferred_element_type=jnp.float32)
            value = value - head.astype(jnp.float32)
        grad[:, h * 128:h * 128 + 128] = (spun * ROOT)[:BLOCK]

    swap_out.wait_recv()
    out[...] = (acc[mine] + other[...]).astype(jnp.bfloat16)

    swap_out.wait_send()
    swap_cot.wait_send()

    @pl.loop(0, 8)
    def _(i):
        swap_tok(i).wait_send()

    drain_a()
    drain_b()
    drain_c()
    drain_d()
    for k in range(1, 8):
        last(k).wait_send()

    @pl.when(odd == 0)
    def _():
        for k in range(9):
            push(yhi, z, zp, k).wait_send()

    @pl.when(odd == 1)
    def _():
        for k in range(6):
            push(yhi, z + 1, zp, k).wait_send()


def on_device(tokens, cotangent, weight_codes, weight_scales, weight_bits, grad_bits):
    table = jnp.asarray(sylvester(), jnp.bfloat16)
    vmem = pl.BlockSpec(memory_space=pltpu.VMEM)
    hbm = pl.BlockSpec(memory_space=pl.ANY)
    dma = pltpu.SemaphoreType.DMA
    bf, f32 = jnp.bfloat16, jnp.float32
    return pl.pallas_call(
        kernel,
        out_shape=(
            jax.ShapeDtypeStruct((256, 256), bf),
            jax.ShapeDtypeStruct((BLOCK, 256), f32),
        ),
        in_specs=[hbm, hbm, vmem, vmem, vmem, vmem, vmem],
        out_specs=(vmem, vmem),
        scratch_shapes=[
            pltpu.VMEM((8, 512, WIN), bf),
            pltpu.VMEM((512, 256), bf),
            pltpu.VMEM((8, WIN, 256), bf),
            pltpu.VMEM((WIN + EDGE, 256), f32),
            pltpu.VMEM((2, 8, 16, 64, 128), f32),
            pltpu.VMEM((2, 2, 3, 16, 64, 128), bf),
            pltpu.VMEM((2, 2, 3, 16, 64, 128), bf),
            pltpu.VMEM((2, 32, 64, 128), f32),
            pltpu.VMEM((2, 2, 3, 4, 64, 128), bf),
            pltpu.VMEM((2, 2, 3, 4, 64, 128), bf),
            pltpu.VMEM((8, 2, 64, 128), f32),
            pltpu.VMEM((8, 2, 64, 128), bf),
            pltpu.VMEM((7, 2, 64, 128), bf),
            pltpu.VMEM((512, 256), f32),
            pltpu.VMEM((256, 256), f32),
            dma((8,)), dma((8,)), dma((8,)), dma((3,)), dma((9,)), dma((8,)),
            dma((2, 2, 3)), dma((2, 2, 3)), dma((2, 2, 3)), dma((2, 2, 3)),
            dma((7,)), dma((7,)), dma((2,)),
        ],
        compiler_params=pltpu.CompilerParams(
            collective_id=0, has_side_effects=True, vmem_limit_bytes=56 * 2**20
        ),
        cost_estimate=pl.CostEstimate(flops=4 * 10**9, bytes_accessed=10**7, transcendentals=0),
    )(
        tokens, cotangent, weight_codes, weight_scales,
        weight_bits.reshape(1, 256), grad_bits.reshape(1, 256), table,
    )


def solution(mesh):
    return jax.shard_map(
        on_device,
        mesh=mesh,
        in_specs=(
            P(("outer", "node"), None),
            P(("outer", "node"), None),
            P("node", None),
            P("node", None),
            P(),
            P(),
        ),
        out_specs=(P(("outer", "node"), None), P(("outer", "node"), None)),
        check_vma=False,
    )
```

time: 479 us -> 71.8 us (0.15)
  waiting for transfers between devices: 237 us -> 0 us
  local copies, waits for them, and re-layouts: 93.1 us -> 4.72 us
  blocking collectives: 74 us -> 0 us
  Pallas kernels: 0 us -> 65.7 us
  matrix products: 51.7 us -> 0 us
  between operations: 14.8 us -> 0.64 us
    reduce_scatter x1 -> x0, waiting for transfers between devices: 226 us -> none  [on_device(): within = lax.psum_scatter(term, 'node', scatter_dimension=0, tiled=True)]
    pallas_call x0 -> x1, Pallas kernels: none -> 65.7 us  [on_device(): pl.pallas_call(kernel, out_shape=(jax.ShapeDtypeStruct((256, 256), bf), j...]
    dot_general x4 -> x0, matrix products: 51.7 us -> none  [the longest x2 38.8 us: rotate(): jnp.einsum('rbi,ij->rbj', blocks, table, precision=lax.Precision.HIGHEST)]
    all_gather x1 -> x0, blocking collectives: 39 us -> none  [on_device(): lax.all_gather(weight_scales.astype(jnp.bfloat16), 'node', axis=0, tiled=...]
    reshape x3 -> x0, local copies, waits for them, and re-layouts: 38.1 us -> none  [the longest x1 15.5 us: rotate(): jnp.einsum('rbi,ij->rbj', blocks, table, precision=lax.Precision.HIGHEST)]
    unnamed x1 -> x0, blocking collectives: 35 us -> none
    mul x1 -> x0, local copies, waits for them, and re-layouts: 28.8 us -> none  [dequantize(): return (blocks * scales[:, :, None]).reshape(height, width)]
    all_gather x1 -> x0, waiting for transfers between devices: 10.5 us -> none  [on_device(): codes = lax.all_gather(weight_codes, 'node', axis=0, tiled=True)]
  transfers between devices with their start and end apart: 4 -> 0, of which waited for: 2 -> 0; matrix products, arithmetic and copies ran while one was open for 30% -> 0% of each run, Pallas kernels for 0% -> 0%
where the time goes in v1:
time: 71.8 us; the launch traced here: 71.1 us
  Pallas kernels  65.7 us (92%)
  local copies, waits for them, and re-layouts  4.72 us (7%)
    pallas_call x1, Pallas kernels, on_device(): pl.pallas_call(kernel, out_shape=(jax.ShapeDtypeStruct((256, 256), bf), j...  65.7 us
    unnamed x3, local copies, waits for them, and re-layouts  4.72 us

profile of v1, /device:TPU:1, one launch (start us, length us, event | category | flops | bytes accessed | tf_op | source)
XLA Modules:
  0.0 71.1 jit_solution(7162769808363371814)
XLA Ops:
  0.6 1.7 %copy.9.scales = f32[928,2]{1,0:T(8,128)} copy(f32[928,2]{0,1:T(2,128)} %param.10) | data formatting | bytes 14848 | tf_op args[3]
  2.3 65.7 %shard_map.86 = (bf16[256,256]{1,0:T(8,128)(2,1)}, f32[58,256]{1,0:T(8,128)}) custom-call(bf16[256,14848]{1,0:T(8,128)(2,1)} %tokens.1, bf16[256,256]{1,0:T(8,128)(2,1)} %cot_in.1, bf16[928,256]{1,0:T(8,128)(2,1)} %codes.1, f32[928,2]{1,0:T(8,128)} %copy.9.scales, s32[1,256]{1,0:T(1,128)} %bitcast.2, s32[1,256]{1,0:T(1,128)} %bitcast.3, ...), custom_call_target="tpu_custom_call" | custom-call | flops 4000000000 | bytes 10000000 | tf_op jit(solution)/shard_map/pallas_call | solution.py:433
  68.0 1.6 %copy.12 = bf16[256,256]{1,0:T(8,128)(2,1)} copy(bf16[256,256]{1,0:T(8,128)(2,1)} %get-tuple-element.4) | data formatting | bytes 262144
  69.6 1.5 %copy.13 = f32[58,256]{1,0:T(8,128)} copy(f32[58,256]{1,0:T(8,128)} %get-tuple-element.5) | data formatting | bytes 118784

commit v2 on v1

v2 whole, which is shorter than its diff:
```python
import math

import jax
import jax.numpy as jnp
import numpy as np
from jax import lax
from jax.experimental import pallas as pl
from jax.experimental.pallas import tpu as pltpu
from jax.sharding import PartitionSpec as P

MESH = pl.DeviceIdType.MESH
SHARD = 928
BLOCK = 58
WIN = 1024
EDGE = 96
HALF = SHARD // 2
END = 128
RUN = HALF - END
ROOT = 1.0 / math.sqrt(128.0)


def sylvester():
    row_index = np.arange(128).reshape(128, 1)
    column_index = np.arange(128).reshape(1, 128)
    parity = np.zeros((128, 128))
    for level in range(7):
        parity = parity + row_index // 2**level % 2 * (column_index // 2**level % 2)
    return 1.0 - 2.0 * (parity % 2)


def kernel(
    tokens, cot_in, codes, scales, wbits, gbits, table,
    out, grad,
    raw, tok, cot, wts, part, s1, d1, r1, s2, d2, r2, s3, d3, acc, other,
    tok_loc, tok_ss, tok_rs, cot_sem, w_ss, w_rs, e_ss, e_rs, ss1, rs1, ss2, rs2, ss3, rs3, o_sem,
):
    o = lax.axis_index("outer")
    n = lax.axis_index("node")
    c = lax.rem(o, 2)
    x = lax.rem(o // 2, 4)
    ylo = o // 8
    yhi = n // 8
    z = lax.rem(n, 8)
    y = yhi * 2 + ylo
    odd = lax.rem(z + c, 2)

    def dev(cc, xx, yy, zz):
        xx, yy, zz = lax.rem(xx + 4, 4), lax.rem(yy + 4, 4), lax.rem(zz + 8, 8)
        return (lax.rem(yy, 2) * 8 + xx * 2 + cc, (yy // 2) * 8 + zz)

    mate = dev(1 - c, x, y, z)
    xp, xm = dev(c, x + 1, y, z), dev(c, x - 1, y, z)
    yp, ym = dev(c, x, y + 1, z), dev(c, x, y - 1, z)
    zp, zm = dev(c, x, y, z + 1), dev(c, x, y, z - 1)
    ypart = dev(c, x, 3 - y, z)
    xodd = lax.rem(x, 2)
    xpair, ypair = dev(c, x + 1 - 2 * xodd, y, z), dev(c, x, y + 1 - 2 * ylo, z)

    zero = jnp.zeros((EDGE, 256), jnp.bfloat16)

    @pl.loop(0, 8)
    def _(i):
        wts[i, pl.ds(0, EDGE)] = zero
        wts[i, pl.ds(WIN - EDGE, EDGE)] = zero

    barrier = pltpu.get_barrier_semaphore()
    peers = [mate, xp, xm, yp, ym] + [dev(c, x, y, z + k) for k in range(1, 8)]
    for p in peers:
        pl.semaphore_signal(barrier, inc=1, device_id=p, device_id_type=MESH)

    def start_of(g):
        return pl.multiple_of(g * SHARD - 32 * lax.rem(g, 4), 128)

    def order(i):
        if isinstance(i, int):
            i = jnp.int32(i)
        first = lax.rem(ylo + i, 2) * 4 + lax.rem(x + 2, 4)
        second = ylo * 4 + lax.rem(x + 1 + i, 4)
        third = (1 - ylo) * 4 + lax.rem(x + 2 + i, 4)
        return jnp.where(i < 2, first, jnp.where(i < 5, second, third))

    def local_tok(gi):
        return pltpu.make_async_copy(
            tokens.at[:, pl.ds(start_of(2 * gi + c), WIN)],
            tok.at[gi, pl.ds(pl.multiple_of(c * 256, 256), 256)],
            tok_loc.at[gi],
        )

    def swap_tok(gi):
        return pltpu.make_async_remote_copy(
            src_ref=tokens.at[:, pl.ds(start_of(2 * gi + 1 - c), WIN)],
            dst_ref=tok.at[gi, pl.ds(pl.multiple_of(c * 256, 256), 256)],
            send_sem=tok_ss.at[gi],
            recv_sem=tok_rs.at[gi],
            device_id=mate,
            device_id_type=MESH,
        )

    cot_mine = cot.at[pl.ds(pl.multiple_of(c * 256, 256), 256)]
    local_cot = pltpu.make_async_copy(cot_in, cot_mine, cot_sem.at[0])
    swap_cot = pltpu.make_async_remote_copy(
        src_ref=cot_in, dst_ref=cot_mine, send_sem=cot_sem.at[1], recv_sem=cot_sem.at[2],
        device_id=mate, device_id_type=MESH,
    )
    local_codes = pltpu.make_async_copy(codes, raw, cot_sem.at[3])

    @pl.when(odd == 0)
    def _():
        local_codes.start()

    local_cot.start()

    @pl.loop(0, 8)
    def _(i):
        local_tok(order(i)).start()

    for h in range(2):
        for i in range(4):
            r1[h, i, pl.ds(HALF, 8)] = jnp.zeros((8, 128), jnp.float32)
    acc[...] = jnp.zeros_like(acc)

    def shard(yy, zz):
        zz = lax.rem(zz + 8, 8)
        slot = yy * 4 + zz // 2
        return slot, 32 * lax.rem(zz, 4)

    def rows_of(yy, zz, first, size):
        slot, base = shard(yy, zz)
        return wts.at[slot, pl.ds(pl.multiple_of(base + first, 16), size)]

    def move(ref, to, ss, rs):
        return pltpu.make_async_remote_copy(
            src_ref=ref, dst_ref=ref, send_sem=ss, recv_sem=rs, device_id=to, device_id_type=MESH
        )

    def push(yy, zz, to, k, i):
        slot, _ = shard(yy, zz)
        skip = (xodd, ylo)[i] * END
        return move(rows_of(yy, zz, i * HALF + skip, RUN), to, w_ss.at[k, i], w_rs.at[slot, i])

    def partner(yy, i):
        slot, _ = shard(yy, z)
        return move(rows_of(yy, z, i * HALF, HALF), ypart, w_ss.at[8, i], w_rs.at[slot, i])

    def swap_end(yy, zz, k, i):
        slot, _ = shard(yy, zz)
        own = (xodd, ylo)[i] * RUN
        return move(rows_of(yy, zz, i * HALF + own, END), (xpair, ypair)[i], e_ss.at[k, i], e_rs.at[slot, i])

    def passing(yy, zz, i, k, to=None, j=0):
        push(yy, zz, zp, 0, i).wait_recv()
        if to is not None:
            push(yy, zz, to, j, i).start()
        swap_end(yy, zz, k, i).start()

    def complete(yy, zz):
        for i in range(2):
            swap_end(yy, zz, 0, i).wait_recv()

    near, far = yhi, 1 - yhi

    def multiply(j):
        dz0 = jnp.where(j < 2, 0, jnp.where(j < 6, jnp.where(lax.rem(j, 2) == 0, -2, 2), 4))
        far0 = jnp.where((j == 1) | (j == 4) | (j == 5) | (j == 7), 1, 0)
        dz1 = jnp.where(j < 4, 1, 3) * jnp.where(lax.rem(j, 2) == 0, -1, 1)
        far1 = jnp.where(lax.rem(j, 4) < 2, 0, 1)
        dz = jnp.where(odd == 0, dz0, dz1)
        off = jnp.where(odd == 0, far0, far1)
        slot = lax.rem(yhi + off, 2) * 4 + lax.rem(z + dz + 8, 8) // 2
        for half in range(2):
            rows = pl.ds(half * 256, 256)
            acc[rows] += jnp.dot(tok[slot, rows], wts[slot], preferred_element_type=jnp.float32)

    @pl.when(odd == 0)
    def _():
        signs = (2 * wbits[...] - 1).astype(jnp.bfloat16)
        factors = (scales[...] * ROOT).T
        local_codes.wait()
        slot = yhi * 4 + z // 2
        base = pl.multiple_of(32 * lax.rem(z, 4), 32)
        for lo in range(0, SHARD, 464):
            for b in range(2):
                cols = pl.ds(b * 128, 128)
                spun = jnp.dot(
                    raw[pl.ds(lo, 464), cols] * signs[:, b * 128:b * 128 + 128], table[...],
                    preferred_element_type=jnp.float32,
                )
                spun = spun * factors[lo:lo + 464, b:b + 1]
                wts[slot, pl.ds(base + lo, 464), cols] = spun.astype(jnp.bfloat16)

    pl.semaphore_wait(barrier, len(peers))

    swap_cot.start()

    @pl.when(odd == 0)
    def _():
        for i in range(2):
            push(near, z, zp, 0, i).start()
            push(near, z, zm, 1, i).start()
            partner(near, i).start()

    @pl.loop(0, 8)
    def _(i):
        swap_tok(order(i)).start()

    local_cot.wait()
    swap_cot.wait_recv()

    def produce(i):
        gi = order(i)
        local_tok(gi).wait()
        swap_tok(gi).wait_recv()
        sums = lax.dot_general(
            tok[gi], cot[...], (((0,), (0,)), ((), ())), preferred_element_type=jnp.float32
        )
        part[0, gi] = sums[:, :128]
        part[1, gi] = sums[:, 128:]

    def ring(level, h):
        along_x = (h == 0) == (level == 1)
        pos = x if along_x else y
        ends = (xp, xm) if along_x else (yp, ym)
        sent, got = (s1, d1) if level == 1 else (s2, d2)
        ssem, rsem = (ss1, rs1) if level == 1 else (ss2, rs2)
        total = r1 if level == 1 else r2

        def copy(way, m):
            return pltpu.make_async_remote_copy(
                src_ref=sent.at[h, way, m], dst_ref=got.at[h, way, m],
                send_sem=ssem.at[h, way, m], recv_sem=rsem.at[h, way, m],
                device_id=ends[way], device_id_type=MESH,
            )

        count = 2 if level == 1 else 4

        def read(dest, half, i):
            if level == 1:
                gi = half * 4 + dest if h == 0 else lax.rem(dest, 2) * 4 + 2 * half + i
                top = 32 * lax.rem(2 * gi + c, 4) + (i if h == 0 else dest // 2) * HALF
                return part[h, gi, pl.ds(pl.multiple_of(top, 16), HALF)]
            block = lax.rem(dest, 2) * 2 + dest // 2 if h == 0 else dest
            return r1[h, block, pl.ds(BLOCK * (half * 4 + i), 64)]

        def send(way, m):
            off = (2, 1, 1)[m] if way == 0 else (2, 3, 3)[m]
            dest = lax.rem(pos + off, 4)
            half = (0, 1, 0)[m] if way == 0 else (1, 0, 1)[m]
            if m == 2:
                copy(way, 0).wait_recv()
            for i in range(count):
                value = read(dest, half, i)
                if m == 2:
                    value = value + got[h, way, 0, i].astype(jnp.float32)
                sent[h, way, m, i] = value.astype(jnp.bfloat16)
            copy(way, m).start()

        def finish():
            for half in range(2):
                a, b = ((0, 2), (1, 1)) if half == 0 else ((0, 1), (1, 2))
                copy(*b).wait_recv()
                copy(*a).wait_recv()
                for i in range(count):
                    value = (
                        read(pos, half, i)
                        + got[(h,) + a + (i,)].astype(jnp.float32)
                        + got[(h,) + b + (i,)].astype(jnp.float32)
                    )
                    if level == 1:
                        r1[h, half * 2 + i, pl.ds(0, HALF)] = value
                    else:
                        r2[half * 4 + i, h] = value

        def drain():
            for way in range(2):
                for m in range(3):
                    copy(way, m).wait_send()

        return send, finish, drain

    send_a, finish_a, drain_a = ring(1, 0)
    send_b, finish_b, drain_b = ring(1, 1)
    send_c, finish_c, drain_c = ring(2, 0)
    send_d, finish_d, drain_d = ring(2, 1)

    def last(h, k):
        to = lax.rem(z + k, 8)
        return pltpu.make_async_remote_copy(
            src_ref=s3.at[h, to], dst_ref=d3.at[h, k - 1],
            send_sem=ss3.at[h, k - 1], recv_sem=rs3.at[h, k - 1],
            device_id=dev(c, x, y, z + k), device_id_type=MESH,
        )

    def last_sends(h):
        for i in range(8):
            s3[h, i] = r2[i, h].astype(jnp.bfloat16)
        for k in (4, 3, 5, 2, 6, 1, 7):
            last(h, k).start()

    def far_own(i):
        partner(far, i).wait_recv()
        push(far, z, zp, 2, i).start()
        push(far, z, zm, 3, i).start()

    def even_near2(i):
        passing(near, z - 2, i, 0, zp, 4)
        passing(near, z + 2, i, 1, zm, 5)

    def even_far2(i):
        passing(far, z - 2, i, 2, zp, 6)
        passing(far, z + 2, i, 3, zm, 7)

    def odd_near1(i):
        passing(near, z - 1, i, 0, zp, 0)
        passing(near, z + 1, i, 1, zm, 1)

    def odd_far1(i):
        passing(far, z - 1, i, 2, zp, 2)
        passing(far, z + 1, i, 3, zm, 3)

    def odd_near3(i):
        passing(near, z - 3, i, 4, zp, 4)
        passing(near, z + 3, i, 5)

    def odd_far3(i):
        passing(far, z + 3, i, 7, zm, 5)
        passing(far, z - 3, i, 6)

    def both(yy, d):
        complete(yy, z - d)
        complete(yy, z + d)

    def ring_start(send, *ms):
        for m in ms:
            send(0, m)
            send(1, m)

    def product(first, last_one):
        pl.loop(first, last_one)(multiply)

    def run(who, act):
        if who == 2:
            act()
        else:
            pl.when(odd == who)(act)

    steps = [
        (2.5, 2, lambda: pl.loop(0, 2)(produce)),
        (2.6, 2, lambda: ring_start(send_a, 0)),
        (5.5, 2, lambda: pl.loop(2, 5)(produce)),
        (5.6, 2, lambda: ring_start(send_b, 0)),
        (8.6, 2, lambda: pl.loop(5, 8)(produce)),
        (8.7, 2, lambda: ring_start(send_a, 1)),
        (8.8, 2, lambda: ring_start(send_b, 1)),
        (10.5, 2, lambda: ring_start(send_a, 2)),
        (13.5, 2, lambda: ring_start(send_b, 2)),
        (21.0, 2, finish_a),
        (21.1, 2, lambda: ring_start(send_c, 0, 1)),
        (23.0, 2, finish_b),
        (23.1, 2, lambda: ring_start(send_d, 0, 1)),
        (24.0, 2, lambda: ring_start(send_c, 2)),
        (26.0, 2, lambda: ring_start(send_d, 2)),
        (26.5, 2, finish_c),
        (26.6, 2, lambda: last_sends(0)),
        (28.5, 2, finish_d),
        (28.6, 2, lambda: last_sends(1)),
        (12.0, 2, lambda: product(0, 2)),
        (17.0, 2, lambda: product(2, 4)),
        (25.0, 2, lambda: product(4, 6)),
        (36.0, 2, lambda: product(6, 8)),
        (4.0, 0, lambda: far_own(0)),
        (6.0, 0, lambda: far_own(1)),
        (8.0, 0, lambda: even_near2(0)),
        (10.0, 0, lambda: even_near2(1)),
        (12.1, 0, lambda: even_far2(0)),
        (14.0, 0, lambda: even_far2(1)),
        (16.9, 0, lambda: both(near, 2)),
        (19.0, 0, lambda: passing(near, z + 4, 0, 4)),
        (21.5, 0, lambda: passing(near, z + 4, 1, 4)),
        (24.9, 0, lambda: both(far, 2)),
        (25.5, 0, lambda: passing(far, z + 4, 0, 5)),
        (28.7, 0, lambda: passing(far, z + 4, 1, 5)),
        (35.8, 0, lambda: complete(near, z + 4)),
        (35.9, 0, lambda: complete(far, z + 4)),
        (3.3, 1, lambda: odd_near1(0)),
        (5.4, 1, lambda: odd_near1(1)),
        (7.0, 1, lambda: odd_far1(0)),
        (9.0, 1, lambda: odd_far1(1)),
        (11.9, 1, lambda: both(near, 1)),
        (14.1, 1, lambda: odd_near3(0)),
        (16.0, 1, lambda: odd_near3(1)),
        (16.9, 1, lambda: both(far, 1)),
        (20.0, 1, lambda: odd_far3(0)),
        (22.0, 1, lambda: odd_far3(1)),
        (24.9, 1, lambda: both(near, 3)),
        (35.9, 1, lambda: both(far, 3)),
    ]
    for _, who, act in sorted(steps, key=lambda step: step[0]):
        run(who, act)

    theirs = pl.ds(pl.multiple_of((1 - c) * 256, 256), 256)
    mine = pl.ds(pl.multiple_of(c * 256, 256), 256)
    swap_out = pltpu.make_async_remote_copy(
        src_ref=acc.at[theirs], dst_ref=other, send_sem=o_sem.at[0], recv_sem=o_sem.at[1],
        device_id=mate, device_id_type=MESH,
    )
    swap_out.start()

    gsigns = (2 * gbits[...] - 1).astype(jnp.float32)
    for h in range(2):
        value = r2[z, h]
        for k in range(1, 8):
            last(h, k).wait_recv()
            value = value + d3[h, k - 1].astype(jnp.float32)
        value = value * gsigns[:, h * 128:h * 128 + 128]
        spun = jnp.zeros((64, 128), jnp.float32)
        for _ in range(3):
            head = value.astype(jnp.bfloat16)
            spun = spun + jnp.dot(head, table[...], preferred_element_type=jnp.float32)
            value = value - head.astype(jnp.float32)
        grad[:, h * 128:h * 128 + 128] = (spun * ROOT)[:BLOCK]

    swap_out.wait_recv()
    out[...] = (acc[mine] + other[...]).astype(jnp.bfloat16)

    swap_out.wait_send()
    swap_cot.wait_send()

    @pl.loop(0, 8)
    def _(i):
        swap_tok(i).wait_send()

    drain_a()
    drain_b()
    drain_c()
    drain_d()
    for h in range(2):
        for k in range(1, 8):
            last(h, k).wait_send()

    def sent_all(pushes, ends):
        for i in range(2):
            for k in range(pushes):
                push(near, z + odd, zp, k, i).wait_send()
            for k in range(ends):
                swap_end(near, z + odd, k, i).wait_send()

    def sent_even():
        for i in range(2):
            partner(near, i).wait_send()
        sent_all(8, 6)

    run(0, sent_even)
    run(1, lambda: sent_all(6, 8))


def place(out_in, grad_in, out, grad):
    out[...] = out_in[...]
    grad[...] = grad_in[...]


def on_device(tokens, cotangent, weight_codes, weight_scales, weight_bits, grad_bits):
    table = jnp.asarray(sylvester(), jnp.bfloat16)
    vmem = pl.BlockSpec(memory_space=pltpu.VMEM)
    hbm = pl.BlockSpec(memory_space=pl.ANY)
    dma = pltpu.SemaphoreType.DMA
    bf, f32 = jnp.bfloat16, jnp.float32
    shapes = (jax.ShapeDtypeStruct((256, 256), bf), jax.ShapeDtypeStruct((BLOCK, 256), f32))
    raw = pl.pallas_call(
        kernel,
        out_shape=shapes,
        in_specs=[hbm, hbm, hbm, vmem, vmem, vmem, vmem],
        out_specs=(vmem, vmem),
        scratch_shapes=[
            pltpu.VMEM((SHARD, 256), bf),
            pltpu.VMEM((8, 512, WIN), bf),
            pltpu.VMEM((512, 256), bf),
            pltpu.VMEM((8, WIN, 256), bf),
            pltpu.VMEM((2, 8, WIN, 128), f32),
            pltpu.VMEM((2, 2, 3, 2, HALF, 128), bf),
            pltpu.VMEM((2, 2, 3, 2, HALF, 128), bf),
            pltpu.VMEM((2, 4, HALF + 8, 128), f32),
            pltpu.VMEM((2, 2, 3, 4, 64, 128), bf),
            pltpu.VMEM((2, 2, 3, 4, 64, 128), bf),
            pltpu.VMEM((8, 2, 64, 128), f32),
            pltpu.VMEM((2, 8, 64, 128), bf),
            pltpu.VMEM((2, 7, 64, 128), bf),
            pltpu.VMEM((512, 256), f32),
            pltpu.VMEM((256, 256), f32),
            dma((8,)), dma((8,)), dma((8,)), dma((4,)),
            dma((9, 2)), dma((8, 2)), dma((8, 2)), dma((8, 2)),
            dma((2, 2, 3)), dma((2, 2, 3)), dma((2, 2, 3)), dma((2, 2, 3)),
            dma((2, 7)), dma((2, 7)), dma((2,)),
        ],
        compiler_params=pltpu.CompilerParams(
            collective_id=0, has_side_effects=True, vmem_limit_bytes=56 * 2**20
        ),
        cost_estimate=pl.CostEstimate(flops=4 * 10**9, bytes_accessed=10**7, transcendentals=0),
    )(
        tokens, cotangent, weight_codes, weight_scales.T,
        weight_bits.reshape(1, 256), grad_bits.reshape(1, 256), table,
    )
    return pl.pallas_call(
        place, out_shape=shapes, in_specs=[vmem, vmem], out_specs=(vmem, vmem)
    )(*raw)


def solution(mesh):
    return jax.shard_map(
        on_device,
        mesh=mesh,
        in_specs=(
            P(("outer", "node"), None),
            P(("outer", "node"), None),
            P("node", None),
            P("node", None),
            P(),
            P(),
        ),
        out_specs=(P(("outer", "node"), None), P(("outer", "node"), None)),
        check_vma=False,
    )
```

time: 71.8 us -> 58.5 us (0.81)
  Pallas kernels: 65.7 us -> 57.7 us
  local copies, waits for them, and re-layouts: 4.72 us -> 0 us
    pallas_call x1 -> x2, Pallas kernels: 65.7 us -> 57.7 us  [the longest x1 56.1 us: on_device(): pl.pallas_call(kernel, out_shape=shapes, in_specs=[hbm, hbm, hbm, vmem, v...]
    unnamed x3 -> x0, local copies, waits for them, and re-layouts: 4.72 us -> none
where the time goes in v2:
time: 58.5 us; the launch traced here: 58.3 us
  Pallas kernels  57.7 us (99%)
  between operations  0.64 us (1%)
    pallas_call x1, Pallas kernels, on_device(): pl.pallas_call(kernel, out_shape=shapes, in_specs=[hbm, hbm, hbm, vmem, v...  56.1 us
    pallas_call x1, Pallas kernels, on_device(): pl.pallas_call(place, out_shape=shapes, in_specs=[vmem, vmem], out_specs=...  1.59 us

profile of v2, /device:TPU:1, one launch (start us, length us, event | category | flops | bytes accessed | tf_op | source)
XLA Modules:
  0.0 58.3 jit_solution(8112265174203250946)
XLA Ops:
  0.6 56.1 %shard_map.86 = (bf16[256,256]{1,0:T(8,128)(2,1)}, f32[58,256]{1,0:T(8,128)}) custom-call(bf16[256,14848]{1,0:T(8,128)(2,1)} %tokens.1, bf16[256,256]{1,0:T(8,128)(2,1)} %cot_in.1, bf16[928,256]{1,0:T(8,128)(2,1)} %codes.1, f32[2,928]{1,0:T(2,128)} %bitcast.3, s32[1,256]{1,0:T(1,128)} %bitcast.4, s32[1,256]{1,0:T(1,128)} %bitcast.5, ...), custom_call_target="tpu_custom_call" | custom-call | flops 4000000000 | bytes 10000000 | tf_op jit(solution)/shard_map/pallas_call | solution.py:468
  56.7 1.6 %shard_map.87 = (bf16[256,256]{1,0:T(8,128)(2,1)}, f32[58,256]{1,0:T(8,128)}) custom-call(bf16[256,256]{1,0:T(8,128)(2,1)} %get-tuple-element.4.out_in, f32[58,256]{1,0:T(8,128)} %get-tuple-element.5.grad_in), custom_call_target="tpu_custom_call" | custom-call | tf_op jit(solution)/shard_map/pallas_call | solution.py:502

commit v3 on v2

--- a/solution.py
+++ b/solution.py
@@ -31,8 +31,8 @@
 def kernel(
     tokens, cot_in, codes, scales, wbits, gbits, table,
     out, grad,
-    raw, tok, cot, wts, part, s1, d1, r1, s2, d2, r2, s3, d3, acc, other,
-    tok_loc, tok_ss, tok_rs, cot_sem, w_ss, w_rs, e_ss, e_rs, ss1, rs1, ss2, rs2, ss3, rs3, o_sem,
+    raw, tok, cot, wts, part, s1, d1, r1, s2, d2, r2, s3, d3, total, other, out_buf, grad_buf,
+    tok_loc, tok_ss, tok_rs, cot_sem, code_sem, w_ss, w_rs, e_ss, e_rs, ss1, rs1, ss2, rs2, ss3, rs3, o_sem,
 ):
     o = lax.axis_index("outer")
     n = lax.axis_index("node")
@@ -102,11 +102,14 @@
         src_ref=cot_in, dst_ref=cot_mine, send_sem=cot_sem.at[1], recv_sem=cot_sem.at[2],
         device_id=mate, device_id_type=MESH,
     )
-    local_codes = pltpu.make_async_copy(codes, raw, cot_sem.at[3])
+    def local_codes(i):
+        rows = pl.ds(i * HALF, HALF)
+        return pltpu.make_async_copy(codes.at[rows], raw.at[rows], code_sem.at[i])
 
     @pl.when(odd == 0)
     def _():
-        local_codes.start()
+        local_codes(0).start()
+        local_codes(1).start()
 
     local_cot.start()
 
@@ -117,7 +120,7 @@
     for h in range(2):
         for i in range(4):
             r1[h, i, pl.ds(HALF, 8)] = jnp.zeros((8, 128), jnp.float32)
-    acc[...] = jnp.zeros_like(acc)
+    total[...] = jnp.zeros_like(total)
 
     def shard(yy, zz):
         zz = lax.rem(zz + 8, 8)
@@ -135,7 +138,7 @@
 
     def push(yy, zz, to, k, i):
         slot, _ = shard(yy, zz)
-        skip = (xodd, ylo)[i] * END
+        skip = (ylo, xodd)[i] * END
         return move(rows_of(yy, zz, i * HALF + skip, RUN), to, w_ss.at[k, i], w_rs.at[slot, i])
 
     def partner(yy, i):
@@ -144,14 +147,13 @@
 
     def swap_end(yy, zz, k, i):
         slot, _ = shard(yy, zz)
-        own = (xodd, ylo)[i] * RUN
-        return move(rows_of(yy, zz, i * HALF + own, END), (xpair, ypair)[i], e_ss.at[k, i], e_rs.at[slot, i])
-
-    def passing(yy, zz, i, k, to=None, j=0):
+        own = (ylo, xodd)[i] * RUN
+        return move(rows_of(yy, zz, i * HALF + own, END), (ypair, xpair)[i], e_ss.at[k, i], e_rs.at[slot, i])
+
+    def passing(yy, zz, i, to=None, j=0):
         push(yy, zz, zp, 0, i).wait_recv()
         if to is not None:
             push(yy, zz, to, j, i).start()
-        swap_end(yy, zz, k, i).start()
 
     def complete(yy, zz):
         for i in range(2):
@@ -159,7 +161,7 @@
 
     near, far = yhi, 1 - yhi
 
-    def multiply(j):
+    def multiply(j, side):
         dz0 = jnp.where(j < 2, 0, jnp.where(j < 6, jnp.where(lax.rem(j, 2) == 0, -2, 2), 4))
         far0 = jnp.where((j == 1) | (j == 4) | (j == 5) | (j == 7), 1, 0)
         dz1 = jnp.where(j < 4, 1, 3) * jnp.where(lax.rem(j, 2) == 0, -1, 1)
@@ -167,39 +169,51 @@
         dz = jnp.where(odd == 0, dz0, dz1)
         off = jnp.where(odd == 0, far0, far1)
         slot = lax.rem(yhi + off, 2) * 4 + lax.rem(z + dz + 8, 8) // 2
-        for half in range(2):
-            rows = pl.ds(half * 256, 256)
-            acc[rows] += jnp.dot(tok[slot, rows], wts[slot], preferred_element_type=jnp.float32)
+        rows = pl.ds(pl.multiple_of(lax.rem(c + side, 2) * 256, 256), 256)
+        total[side] += jnp.dot(tok[slot, rows], wts[slot], preferred_element_type=jnp.float32)
+
+    def rotate_half(i):
+        signs = (2 * wbits[...] - 1).astype(jnp.bfloat16)
+        factors = (scales[...] * ROOT).T
+        local_codes(i).wait()
+        slot, base = shard(near, z)
+        lo = i * HALF
+        for b in range(2):
+            cols = pl.ds(b * 128, 128)
+            spun = jnp.dot(
+                raw[pl.ds(lo, HALF), cols] * signs[:, b * 128:b * 128 + 128], table[...],
+                preferred_element_type=jnp.float32,
+            )
+            spun = spun * factors[lo:lo + HALF, b:b + 1]
+            wts[slot, pl.ds(pl.multiple_of(base + lo, 16), HALF), cols] = spun.astype(jnp.bfloat16)
 
     @pl.when(odd == 0)
     def _():
-        signs = (2 * wbits[...] - 1).astype(jnp.bfloat16)
-        factors = (scales[...] * ROOT).T
-        local_codes.wait()
-        slot = yhi * 4 + z // 2
-        base = pl.multiple_of(32 * lax.rem(z, 4), 32)
-        for lo in range(0, SHARD, 464):
-            for b in range(2):
-                cols = pl.ds(b * 128, 128)
-                spun = jnp.dot(
-                    raw[pl.ds(lo, 464), cols] * signs[:, b * 128:b * 128 + 128], table[...],
-                    preferred_element_type=jnp.float32,
-                )
-                spun = spun * factors[lo:lo + 464, b:b + 1]
-                wts[slot, pl.ds(base + lo, 464), cols] = spun.astype(jnp.bfloat16)
+        rotate_half(0)
 
     pl.semaphore_wait(barrier, len(peers))
 
     swap_cot.start()
+
+    def push_own(i):
+        push(near, z, zp, 0, i).start()
+        push(near, z, zm, 1, i).start()
+        partner(near, i).start()
 
     @pl.when(odd == 0)
     def _():
-        for i in range(2):
-            push(near, z, zp, 0, i).start()
-            push(near, z, zm, 1, i).start()
-            partner(near, i).start()
-
-    @pl.loop(0, 8)
+        push_own(0)
+
+    @pl.loop(0, 2)
+    def _(i):
+        swap_tok(order(i)).start()
+
+    @pl.when(odd == 0)
+    def _():
+        rotate_half(1)
+        push_own(1)
+
+    @pl.loop(2, 8)
     def _(i):
         swap_tok(order(i)).start()
 
@@ -224,21 +238,24 @@
         ssem, rsem = (ss1, rs1) if level == 1 else (ss2, rs2)
         total = r1 if level == 1 else r2
 
-        def copy(way, m):
+        def copy(way, m, piece=None):
+            place_of = (h, way, m) if piece is None else (h, way, 2, piece)
             return pltpu.make_async_remote_copy(
-                src_ref=sent.at[h, way, m], dst_ref=got.at[h, way, m],
+                src_ref=sent.at[place_of], dst_ref=got.at[place_of],
                 send_sem=ssem.at[h, way, m], recv_sem=rsem.at[h, way, m],
                 device_id=ends[way], device_id_type=MESH,
             )
 
         count = 2 if level == 1 else 4
+        first = 1 - yhi if h == 0 else 0
+        turn = (first, 1 - first)
 
         def read(dest, half, i):
             if level == 1:
-                gi = half * 4 + dest if h == 0 else lax.rem(dest, 2) * 4 + 2 * half + i
+                gi = half * 4 + dest if h == 0 else lax.rem(dest, 2) * 4 + lax.rem(x + 2 + 2 * half + i, 4)
                 top = 32 * lax.rem(2 * gi + c, 4) + (i if h == 0 else dest // 2) * HALF
                 return part[h, gi, pl.ds(pl.multiple_of(top, 16), HALF)]
-            block = lax.rem(dest, 2) * 2 + dest // 2 if h == 0 else dest
+            block = lax.rem(dest, 2) * 2 + dest // 2 if h == 0 else lax.rem(dest - x + 6, 4)
             return r1[h, block, pl.ds(BLOCK * (half * 4 + i), 64)]
 
         def send(way, m):
@@ -247,19 +264,26 @@
             half = (0, 1, 0)[m] if way == 0 else (1, 0, 1)[m]
             if m == 2:
                 copy(way, 0).wait_recv()
-            for i in range(count):
+            for j in range(count):
+                i = turn[j] if level == 1 and m == 2 else j
                 value = read(dest, half, i)
                 if m == 2:
                     value = value + got[h, way, 0, i].astype(jnp.float32)
                 sent[h, way, m, i] = value.astype(jnp.bfloat16)
-            copy(way, m).start()
-
-        def finish():
+                if level == 1 and m == 2:
+                    copy(way, 2 + j, i).start()
+            if level == 2 or m < 2:
+                copy(way, m).start()
+
+        def finish(j=0):
             for half in range(2):
                 a, b = ((0, 2), (1, 1)) if half == 0 else ((0, 1), (1, 2))
-                copy(*b).wait_recv()
-                copy(*a).wait_recv()
-                for i in range(count):
+                for way, m in (b, a):
+                    if level == 1 and m == 2:
+                        copy(way, 2 + j, turn[j]).wait_recv()
+                    elif j == 0:
+                        copy(way, m).wait_recv()
+                for i in ((turn[j],) if level == 1 else range(count)):
                     value = (
                         read(pos, half, i)
                         + got[(h,) + a + (i,)].astype(jnp.float32)
@@ -272,8 +296,8 @@
 
         def drain():
             for way in range(2):
-                for m in range(3):
-                    copy(way, m).wait_send()
+                for m in range(4 if level == 1 else 3):
+                    copy(way, m, turn[m - 2] if level == 1 and m > 1 else None).wait_send()
 
         return send, finish, drain
 
@@ -301,29 +325,13 @@
         push(far, z, zp, 2, i).start()
         push(far, z, zm, 3, i).start()
 
-    def even_near2(i):
-        passing(near, z - 2, i, 0, zp, 4)
-        passing(near, z + 2, i, 1, zm, 5)
-
-    def even_far2(i):
-        passing(far, z - 2, i, 2, zp, 6)
-        passing(far, z + 2, i, 3, zm, 7)
-
-    def odd_near1(i):
-        passing(near, z - 1, i, 0, zp, 0)
-        passing(near, z + 1, i, 1, zm, 1)
-
-    def odd_far1(i):
-        passing(far, z - 1, i, 2, zp, 2)
-        passing(far, z + 1, i, 3, zm, 3)
-
-    def odd_near3(i):
-        passing(near, z - 3, i, 4, zp, 4)
-        passing(near, z + 3, i, 5)
-
-    def odd_far3(i):
-        passing(far, z + 3, i, 7, zm, 5)
-        passing(far, z - 3, i, 6)
+    def pass_pair(yy, d, i, first, second):
+        passing(yy, z - d, i, *first)
+        passing(yy, z + d, i, *second)
+
+    def ends(yy, d, k, i):
+        swap_end(yy, z - d, k, i).start()
+        swap_end(yy, z + d, k + 1, i).start()
 
     def both(yy, d):
         complete(yy, z - d)
@@ -334,8 +342,9 @@
             send(0, m)
             send(1, m)
 
-    def product(first, last_one):
-        pl.loop(first, last_one)(multiply)
+    def product(first, last_one, *sides):
+        for side in sides:
+            pl.loop(first, last_one)(lambda j: multiply(j, side))
 
     def run(who, act):
         if who == 2:
@@ -343,67 +352,89 @@
         else:
             pl.when(odd == who)(act)
 
+    swap_out = pltpu.make_async_remote_copy(
+        src_ref=total.at[1], dst_ref=other, send_sem=o_sem.at[0], recv_sem=o_sem.at[1],
+        device_id=mate, device_id_type=MESH,
+    )
+    write_out = pltpu.make_async_copy(out_buf, out, o_sem.at[2])
+    write_grad = pltpu.make_async_copy(grad_buf, grad, o_sem.at[3])
+
     steps = [
         (2.5, 2, lambda: pl.loop(0, 2)(produce)),
         (2.6, 2, lambda: ring_start(send_a, 0)),
-        (5.5, 2, lambda: pl.loop(2, 5)(produce)),
-        (5.6, 2, lambda: ring_start(send_b, 0)),
-        (8.6, 2, lambda: pl.loop(5, 8)(produce)),
-        (8.7, 2, lambda: ring_start(send_a, 1)),
-        (8.8, 2, lambda: ring_start(send_b, 1)),
+        (3.3, 1, lambda: pass_pair(near, 1, 0, (zp, 0), (zm, 1))),
+        (3.33, 1, lambda: ends(near, 1, 0, 0)),
+        (4.5, 2, lambda: pl.loop(2, 3)(produce)),
+        (5.4, 1, lambda: pass_pair(near, 1, 1, (zp, 0), (zm, 1))),
+        (5.43, 1, lambda: ends(near, 1, 0, 1)),
+        (5.98, 2, lambda: send_b(0, 0)),
+        (6.0, 2, lambda: pl.loop(3, 5)(produce)),
+        (6.1, 2, lambda: send_b(1, 0)),
+        (6.78, 0, lambda: far_own(0)),
+        (7.0, 1, lambda: pass_pair(far, 1, 0, (zp, 2), (zm, 3))),
+        (7.03, 1, lambda: ends(far, 1, 2, 0)),
+        (8.78, 0, lambda: far_own(1)),
+        (9.0, 2, lambda: pl.loop(5, 8)(produce)),
+        (9.01, 1, lambda: pass_pair(far, 1, 1, (zp, 2), (zm, 3))),
+        (9.03, 1, lambda: ends(far, 1, 2, 1)),
+        (9.1, 2, lambda: ring_start(send_a, 1)),
+        (9.2, 2, lambda: ring_start(send_b, 1)),
         (10.5, 2, lambda: ring_start(send_a, 2)),
+        (10.78, 0, lambda: pass_pair(near, 2, 0, (zp, 4), (zm, 5))),
+        (10.8, 0, lambda: ends(near, 2, 0, 0)),
+        (12.78, 0, lambda: pass_pair(near, 2, 1, (zp, 4), (zm, 5))),
+        (12.8, 0, lambda: ends(near, 2, 0, 1)),
         (13.5, 2, lambda: ring_start(send_b, 2)),
-        (21.0, 2, finish_a),
-        (21.1, 2, lambda: ring_start(send_c, 0, 1)),
-        (23.0, 2, finish_b),
-        (23.1, 2, lambda: ring_start(send_d, 0, 1)),
-        (24.0, 2, lambda: ring_start(send_c, 2)),
-        (26.0, 2, lambda: ring_start(send_d, 2)),
-        (26.5, 2, finish_c),
-        (26.6, 2, lambda: last_sends(0)),
+        (14.1, 1, lambda: pass_pair(near, 3, 0, (zp, 4), ())),
+        (14.13, 1, lambda: ends(near, 3, 4, 0)),
+        (14.88, 0, lambda: pass_pair(far, 2, 0, (zp, 6), (zm, 7))),
+        (14.9, 0, lambda: ends(far, 2, 2, 0)),
+        (15.7, 1, lambda: both(far, 1)),
+        (16.0, 1, lambda: pass_pair(near, 3, 1, (zp, 4), ())),
+        (16.03, 1, lambda: ends(near, 3, 4, 1)),
+        (16.78, 0, lambda: pass_pair(far, 2, 1, (zp, 6), (zm, 7))),
+        (16.8, 0, lambda: ends(far, 2, 2, 1)),
+        (16.81, 1, lambda: both(near, 1)),
+        (16.9, 0, lambda: both(near, 2)),
+        (17.0, 2, lambda: product(0, 4, 1, 0)),
+        (19.5, 2, finish_a),
+        (19.6, 2, lambda: ring_start(send_c, 0)),
+        (20.5, 2, lambda: finish_a(1)),
+        (20.6, 2, lambda: ring_start(send_c, 1)),
+        (21.5, 2, finish_b),
+        (21.6, 2, lambda: ring_start(send_d, 0)),
+        (21.78, 0, lambda: passing(near, z + 4, 0)),
+        (21.8, 0, lambda: swap_end(near, z + 4, 4, 0).start()),
+        (21.9, 1, lambda: pass_pair(far, 3, 1, (), (zm, 5))),
+        (21.93, 1, lambda: ends(far, 3, 6, 1)),
+        (22.02, 1, lambda: pass_pair(far, 3, 0, (), (zm, 5))),
+        (22.04, 1, lambda: ends(far, 3, 6, 0)),
+        (22.4, 2, lambda: ring_start(send_c, 2)),
+        (23.0, 2, lambda: finish_b(1)),
+        (23.1, 2, lambda: ring_start(send_d, 1)),
+        (24.28, 0, lambda: passing(near, z + 4, 1)),
+        (24.3, 0, lambda: swap_end(near, z + 4, 4, 1).start()),
+        (24.5, 2, lambda: ring_start(send_d, 2)),
+        (24.9, 0, lambda: both(far, 2)),
+        (24.91, 1, lambda: both(near, 3)),
+        (25.0, 2, lambda: product(4, 6, 1, 0)),
+        (25.5, 2, finish_c),
+        (25.52, 2, lambda: last_sends(0)),
+        (28.2, 0, lambda: passing(far, z + 4, 0)),
+        (28.22, 0, lambda: swap_end(far, z + 4, 5, 0).start()),
         (28.5, 2, finish_d),
         (28.6, 2, lambda: last_sends(1)),
-        (12.0, 2, lambda: product(0, 2)),
-        (17.0, 2, lambda: product(2, 4)),
-        (25.0, 2, lambda: product(4, 6)),
-        (36.0, 2, lambda: product(6, 8)),
-        (4.0, 0, lambda: far_own(0)),
-        (6.0, 0, lambda: far_own(1)),
-        (8.0, 0, lambda: even_near2(0)),
-        (10.0, 0, lambda: even_near2(1)),
-        (12.1, 0, lambda: even_far2(0)),
-        (14.0, 0, lambda: even_far2(1)),
-        (16.9, 0, lambda: both(near, 2)),
-        (19.0, 0, lambda: passing(near, z + 4, 0, 4)),
-        (21.5, 0, lambda: passing(near, z + 4, 1, 4)),
-        (24.9, 0, lambda: both(far, 2)),
-        (25.5, 0, lambda: passing(far, z + 4, 0, 5)),
-        (28.7, 0, lambda: passing(far, z + 4, 1, 5)),
+        (30.66, 0, lambda: passing(far, z + 4, 1)),
+        (30.68, 0, lambda: swap_end(far, z + 4, 5, 1).start()),
         (35.8, 0, lambda: complete(near, z + 4)),
         (35.9, 0, lambda: complete(far, z + 4)),
-        (3.3, 1, lambda: odd_near1(0)),
-        (5.4, 1, lambda: odd_near1(1)),
-        (7.0, 1, lambda: odd_far1(0)),
-        (9.0, 1, lambda: odd_far1(1)),
-        (11.9, 1, lambda: both(near, 1)),
-        (14.1, 1, lambda: odd_near3(0)),
-        (16.0, 1, lambda: odd_near3(1)),
-        (16.9, 1, lambda: both(far, 1)),
-        (20.0, 1, lambda: odd_far3(0)),
-        (22.0, 1, lambda: odd_far3(1)),
-        (24.9, 1, lambda: both(near, 3)),
-        (35.9, 1, lambda: both(far, 3)),
+        (35.91, 1, lambda: both(far, 3)),
+        (36.0, 2, lambda: product(6, 8, 1)),
+        (36.1, 2, lambda: swap_out.start()),
+        (38.95, 2, lambda: product(6, 8, 0)),
     ]
     for _, who, act in sorted(steps, key=lambda step: step[0]):
         run(who, act)
-
-    theirs = pl.ds(pl.multiple_of((1 - c) * 256, 256), 256)
-    mine = pl.ds(pl.multiple_of(c * 256, 256), 256)
-    swap_out = pltpu.make_async_remote_copy(
-        src_ref=acc.at[theirs], dst_ref=other, send_sem=o_sem.at[0], recv_sem=o_sem.at[1],
-        device_id=mate, device_id_type=MESH,
-    )
-    swap_out.start()
 
     gsigns = (2 * gbits[...] - 1).astype(jnp.float32)
     for h in range(2):
@@ -417,10 +448,12 @@
             head = value.astype(jnp.bfloat16)
             spun = spun + jnp.dot(head, table[...], preferred_element_type=jnp.float32)
             value = value - head.astype(jnp.float32)
-        grad[:, h * 128:h * 128 + 128] = (spun * ROOT)[:BLOCK]
+        grad_buf[:, h * 128:h * 128 + 128] = (spun * ROOT)[:BLOCK]
+    write_grad.start()
 
     swap_out.wait_recv()
-    out[...] = (acc[mine] + other[...]).astype(jnp.bfloat16)
+    out_buf[...] = (total[0] + other[...]).astype(jnp.bfloat16)
+    write_out.start()
 
     swap_out.wait_send()
     swap_cot.wait_send()
@@ -451,6 +484,8 @@
 
     run(0, sent_even)
     run(1, lambda: sent_all(6, 8))
+    write_grad.wait()
+    write_out.wait()
 
 
 def place(out_in, grad_in, out, grad):
@@ -469,7 +504,7 @@
         kernel,
         out_shape=shapes,
         in_specs=[hbm, hbm, hbm, vmem, vmem, vmem, vmem],
-        out_specs=(vmem, vmem),
+        out_specs=(hbm, hbm),
         scratch_shapes=[
             pltpu.VMEM((SHARD, 256), bf),
             pltpu.VMEM((8, 512, WIN), bf),
@@ -484,12 +519,14 @@
             pltpu.VMEM((8, 2, 64, 128), f32),
             pltpu.VMEM((2, 8, 64, 128), bf),
             pltpu.VMEM((2, 7, 64, 128), bf),
-            pltpu.VMEM((512, 256), f32),
+            pltpu.VMEM((2, 256, 256), f32),
             pltpu.VMEM((256, 256), f32),
-            dma((8,)), dma((8,)), dma((8,)), dma((4,)),
+            pltpu.VMEM((256, 256), bf),
+            pltpu.VMEM((BLOCK, 256), f32),
+            dma((8,)), dma((8,)), dma((8,)), dma((3,)), dma((2,)),
             dma((9, 2)), dma((8, 2)), dma((8, 2)), dma((8, 2)),
-            dma((2, 2, 3)), dma((2, 2, 3)), dma((2, 2, 3)), dma((2, 2, 3)),
-            dma((2, 7)), dma((2, 7)), dma((2,)),
+            dma((2, 2, 4)), dma((2, 2, 4)), dma((2, 2, 3)), dma((2, 2, 3)),
+            dma((2, 7)), dma((2, 7)), dma((4,)),
         ],
         compiler_params=pltpu.CompilerParams(
             collective_id=0, has_side_effects=True, vmem_limit_bytes=56 * 2**20

time: 58.5 us -> 56.3 us (0.962)
  Pallas kernels: 57.7 us -> 55.5 us
    pallas_call x1, Pallas kernels: 56.1 us -> 53.9 us  [on_device(): pl.pallas_call(kernel, out_shape=shapes, in_specs=[hbm, hbm, hbm, vmem, v...]
where the time goes in v3:
time: 56.3 us; the launch traced here: 56.1 us
  Pallas kernels  55.5 us (99%)
  between operations  0.64 us (1%)
    pallas_call x1, Pallas kernels, on_device(): pl.pallas_call(kernel, out_shape=shapes, in_specs=[hbm, hbm, hbm, vmem, v...  53.9 us
    pallas_call x1, Pallas kernels, on_device(): pl.pallas_call(place, out_shape=shapes, in_specs=[vmem, vmem], out_specs=...  1.59 us

profile of v3, /device:TPU:1, one launch (start us, length us, event | category | flops | bytes accessed | tf_op | source)
XLA Modules:
  0.0 56.1 jit_solution(7809564343439097087)
XLA Ops:
  0.6 53.9 %shard_map.86 = (bf16[256,256]{1,0:T(8,128)(2,1)}, f32[58,256]{1,0:T(8,128)}) custom-call(bf16[256,14848]{1,0:T(8,128)(2,1)} %tokens.1, bf16[256,256]{1,0:T(8,128)(2,1)} %cot_in.1, bf16[928,256]{1,0:T(8,128)(2,1)} %codes.1, f32[2,928]{1,0:T(2,128)} %bitcast.3, s32[1,256]{1,0:T(1,128)} %bitcast.4, s32[1,256]{1,0:T(1,128)} %bitcast.5, ...), custom_call_target="tpu_custom_call" | custom-call | flops 4000000000 | bytes 10000000 | tf_op jit(solution)/shard_map/pallas_call | solution.py:503
  54.5 1.6 %shard_map.87 = (bf16[256,256]{1,0:T(8,128)(2,1)}, f32[58,256]{1,0:T(8,128)}) custom-call(bf16[256,256]{1,0:T(8,128)(2,1)} %get-tuple-element.4.out_in, f32[58,256]{1,0:T(8,128)} %get-tuple-element.5.grad_in), custom_call_target="tpu_custom_call" | custom-call | tf_op jit(solution)/shard_map/pallas_call | solution.py:539

commit v4 on v3

--- a/solution.py
+++ b/solution.py
@@ -29,10 +29,10 @@
 
 
 def kernel(
-    tokens, cot_in, codes, scales, wbits, gbits, table,
+    tokens, cot_in, codes, scales_in, wbits_in, gbits_in, table_in,
     out, grad,
-    raw, tok, cot, wts, part, s1, d1, r1, s2, d2, r2, s3, d3, total, other, out_buf, grad_buf,
-    tok_loc, tok_ss, tok_rs, cot_sem, code_sem, w_ss, w_rs, e_ss, e_rs, ss1, rs1, ss2, rs2, ss3, rs3, o_sem,
+    scales, wbits, gbits, table, raw, tok, cot, wts, part, s1, d1, r1, s2, d2, r2, s3, d3, total, other, out_buf, grad_buf,
+    tok_loc, tok_ss, tok_rs, cot_sem, code_sem, small_sem, w_ss, w_rs, e_ss, e_rs, ss1, rs1, ss2, rs2, ss3, rs3, o_sem,
 ):
     o = lax.axis_index("outer")
     n = lax.axis_index("node")
@@ -56,6 +56,13 @@
     xodd = lax.rem(x, 2)
     xpair, ypair = dev(c, x + 1 - 2 * xodd, y, z), dev(c, x, y + 1 - 2 * ylo, z)
 
+    small = [
+        pltpu.make_async_copy(source, target, small_sem.at[i])
+        for i, (source, target) in enumerate(
+            ((scales_in, scales), (wbits_in, wbits), (gbits_in, gbits), (table_in, table))
+        )
+    ]
+
     zero = jnp.zeros((EDGE, 256), jnp.bfloat16)
 
     @pl.loop(0, 8)
@@ -67,6 +74,9 @@
     peers = [mate, xp, xm, yp, ym] + [dev(c, x, y, z + k) for k in range(1, 8)]
     for p in peers:
         pl.semaphore_signal(barrier, inc=1, device_id=p, device_id_type=MESH)
+
+    for copy_in in small:
+        copy_in.start()
 
     def start_of(g):
         return pl.multiple_of(g * SHARD - 32 * lax.rem(g, 4), 128)
@@ -186,6 +196,9 @@
             )
             spun = spun * factors[lo:lo + HALF, b:b + 1]
             wts[slot, pl.ds(pl.multiple_of(base + lo, 16), HALF), cols] = spun.astype(jnp.bfloat16)
+
+    for copy_in in small:
+        copy_in.wait()
 
     @pl.when(odd == 0)
     def _():
@@ -503,9 +516,13 @@
     raw = pl.pallas_call(
         kernel,
         out_shape=shapes,
-        in_specs=[hbm, hbm, hbm, vmem, vmem, vmem, vmem],
+        in_specs=[hbm] * 7,
         out_specs=(hbm, hbm),
         scratch_shapes=[
+            pltpu.VMEM((2, SHARD), f32),
+            pltpu.VMEM((1, 256), jnp.int32),
+            pltpu.VMEM((1, 256), jnp.int32),
+            pltpu.VMEM((128, 128), bf),
             pltpu.VMEM((SHARD, 256), bf),
             pltpu.VMEM((8, 512, WIN), bf),
             pltpu.VMEM((512, 256), bf),
@@ -523,7 +540,7 @@
             pltpu.VMEM((256, 256), f32),
             pltpu.VMEM((256, 256), bf),
             pltpu.VMEM((BLOCK, 256), f32),
-            dma((8,)), dma((8,)), dma((8,)), dma((3,)), dma((2,)),
+            dma((8,)), dma((8,)), dma((8,)), dma((3,)), dma((2,)), dma((4,)),
             dma((9, 2)), dma((8, 2)), dma((8, 2)), dma((8, 2)),
             dma((2, 2, 4)), dma((2, 2, 4)), dma((2, 2, 3)), dma((2, 2, 3)),
             dma((2, 7)), dma((2, 7)), dma((4,)),

time: 56.3 us -> 55.5 us (0.986)
  Pallas kernels: 55.5 us -> 54.7 us
    pallas_call x1, Pallas kernels: 53.9 us -> 53.1 us  [on_device(): pl.pallas_call(kernel, out_shape=shapes, in_specs=[hbm] * 7, out_specs=(h...]
where the time goes in v4:
time: 55.5 us; the launch traced here: 55.4 us
  Pallas kernels  54.7 us (99%)
  between operations  0.64 us (1%)
    pallas_call x1, Pallas kernels, on_device(): pl.pallas_call(kernel, out_shape=shapes, in_specs=[hbm] * 7, out_specs=(h...  53.1 us
    pallas_call x1, Pallas kernels, on_device(): pl.pallas_call(place, out_shape=shapes, in_specs=[vmem, vmem], out_specs=...  1.59 us

profile of v4, /device:TPU:1, one launch (start us, length us, event | category | flops | bytes accessed | tf_op | source)
XLA Modules:
  0.0 55.4 jit_solution(1259180198419591756)
XLA Ops:
  0.6 53.1 %shard_map.86 = (bf16[256,256]{1,0:T(8,128)(2,1)}, f32[58,256]{1,0:T(8,128)}) custom-call(bf16[256,14848]{1,0:T(8,128)(2,1)} %tokens.1, bf16[256,256]{1,0:T(8,128)(2,1)} %cot_in.1, bf16[928,256]{1,0:T(8,128)(2,1)} %codes.1, f32[2,928]{1,0:T(2,128)} %bitcast.3, s32[1,256]{1,0:T(1,128)} %bitcast.4, s32[1,256]{1,0:T(1,128)} %bitcast.5, ...), custom_call_target="tpu_custom_call" | custom-call | flops 4000000000 | bytes 10000000 | tf_op jit(solution)/shard_map/pallas_call | solution.py:516
  53.8 1.6 %shard_map.87 = (bf16[256,256]{1,0:T(8,128)(2,1)}, f32[58,256]{1,0:T(8,128)}) custom-call(bf16[256,256]{1,0:T(8,128)(2,1)} %get-tuple-element.4.out_in, f32[58,256]{1,0:T(8,128)} %get-tuple-element.5.grad_in), custom_call_target="tpu_custom_call" | custom-call | tf_op jit(solution)/shard_map/pallas_call | solution.py:556

commit v5 on v4

--- a/solution.py
+++ b/solution.py
@@ -63,6 +63,18 @@
         )
     ]
 
+    def local_codes(i):
+        rows = pl.ds(i * HALF, HALF)
+        return pltpu.make_async_copy(codes.at[rows], raw.at[rows], code_sem.at[i])
+
+    @pl.when(odd == 0)
+    def _():
+        local_codes(0).start()
+        local_codes(1).start()
+
+    for copy_in in small:
+        copy_in.start()
+
     zero = jnp.zeros((EDGE, 256), jnp.bfloat16)
 
     @pl.loop(0, 8)
@@ -74,9 +86,6 @@
     peers = [mate, xp, xm, yp, ym] + [dev(c, x, y, z + k) for k in range(1, 8)]
     for p in peers:
         pl.semaphore_signal(barrier, inc=1, device_id=p, device_id_type=MESH)
-
-    for copy_in in small:
-        copy_in.start()
 
     def start_of(g):
         return pl.multiple_of(g * SHARD - 32 * lax.rem(g, 4), 128)
@@ -112,15 +121,6 @@
         src_ref=cot_in, dst_ref=cot_mine, send_sem=cot_sem.at[1], recv_sem=cot_sem.at[2],
         device_id=mate, device_id_type=MESH,
     )
-    def local_codes(i):
-        rows = pl.ds(i * HALF, HALF)
-        return pltpu.make_async_copy(codes.at[rows], raw.at[rows], code_sem.at[i])
-
-    @pl.when(odd == 0)
-    def _():
-        local_codes(0).start()
-        local_codes(1).start()
-
     local_cot.start()
 
     @pl.loop(0, 8)

time: 55.5 us -> 55.6 us (level)
  no operation moved by 1% of the time
where the time goes in v5:
time: 55.6 us; the launch traced here: 55.4 us
  Pallas kernels  54.7 us (98%)
  between operations  0.64 us (1%)
    pallas_call x1, Pallas kernels, on_device(): pl.pallas_call(kernel, out_shape=shapes, in_specs=[hbm] * 7, out_specs=(h...  53.1 us
    pallas_call x1, Pallas kernels, on_device(): pl.pallas_call(place, out_shape=shapes, in_specs=[vmem, vmem], out_specs=...  1.59 us

profile of v5, /device:TPU:1, one launch (start us, length us, event | category | flops | bytes accessed | tf_op | source)
XLA Modules:
  0.0 55.4 jit_solution(11743638376220369249)
XLA Ops:
  0.6 53.1 %shard_map.86 = (bf16[256,256]{1,0:T(8,128)(2,1)}, f32[58,256]{1,0:T(8,128)}) custom-call(bf16[256,14848]{1,0:T(8,128)(2,1)} %tokens.1, bf16[256,256]{1,0:T(8,128)(2,1)} %cot_in.1, bf16[928,256]{1,0:T(8,128)(2,1)} %codes.1, f32[2,928]{1,0:T(2,128)} %bitcast.3, s32[1,256]{1,0:T(1,128)} %bitcast.4, s32[1,256]{1,0:T(1,128)} %bitcast.5, ...), custom_call_target="tpu_custom_call" | custom-call | flops 4000000000 | bytes 10000000 | tf_op jit(solution)/shard_map/pallas_call | solution.py:516
  53.8 1.6 %shard_map.87 = (bf16[256,256]{1,0:T(8,128)(2,1)}, f32[58,256]{1,0:T(8,128)}) custom-call(bf16[256,256]{1,0:T(8,128)(2,1)} %get-tuple-element.4.out_in, f32[58,256]{1,0:T(8,128)} %get-tuple-element.5.grad_in), custom_call_target="tpu_custom_call" | custom-call | tf_op jit(solution)/shard_map/pallas_call | solution.py:556
